TPU v7x, 32 devices: a whole 2x2x4 slice. The times are simulated.
32 devices in a mesh: chain: 4 (over z), param: 8 (over y, x, core).
Axes of the slice: x: 2, y: 2, z: 4, core: 2. Of those that a mesh axis runs over, the one named last changes fastest.
Arguments:
- spins: int32 [128, 256, 4], P(('chain', 'param')), may hold values from 0 to 1
- local_energy: float32 [128], replicated, may hold values from -24 to 24
- embed_weight: float32 [4, 256], replicated, may hold values from -3 to 3
- position: bfloat16 [256, 256], replicated, may hold values from -6 to 6
- value_weight: bfloat16 [256, 256], replicated, may hold values from -0.375 to 0.375
- mixing: bfloat16 [8, 256, 256], replicated, may hold values from -0.375 to 0.375
- out_weight: bfloat16 [256, 256], replicated, may hold values from -0.375 to 0.375
- up_weight: bfloat16 [256, 1024], replicated, may hold values from -0.375 to 0.375
- down_weight: bfloat16 [1024, 256], replicated, may hold values from -0.1875 to 0.1875
- readout: float32 [256], replicated, may hold values from -6 to 6
Outputs:
- up_update: float32 [256, 1024], P('chain', 'param')
- down_update: float32 [1024, 256], P('param', 'chain')
- sample_weights: float32 [128], replicated
All inputs are finite; a program needn't handle non-finite values.
Results may differ from a plain program's by a relative error of at most 0.018.
Values may be sent and summed in bfloat16 or wider, within the bound.
A program may use at most 128 MiB of HBM per device.

v0:
```python
import math

import jax
import jax.numpy as jnp
from jax import lax
from jax.sharding import PartitionSpec as P

damping = 0.05


def layer_norm(hidden_state):
    average = jnp.mean(hidden_state, axis=-1, keepdims=True)
    centred = hidden_state - average
    spread = jnp.mean(centred * centred, axis=-1, keepdims=True)
    return centred * lax.rsqrt(spread + 1e-05)


def project(operand, weights):
    return lax.dot_general(
        operand,
        weights,
        (((operand.ndim - 1,), (0,)), ((), ())),
        preferred_element_type=jnp.float32,
    )


def center_rows(jacobian, total):
    jac_wide = jacobian.astype(jnp.float32)
    return (jac_wide - jnp.mean(jac_wide, axis=0)) / math.sqrt(total)


def gram_of(centred, total):
    flat = centred.reshape(total, -1)
    return lax.dot_general(
        flat,
        flat,
        (((1,), (1,)), ((), ())),
        precision=lax.Precision.HIGHEST,
        preferred_element_type=jnp.float32,
    )


def solve_weights(gram, local_energy, total):
    scale = jnp.trace(gram) / total
    system = gram + damping * scale * jnp.eye(total, dtype=jnp.float32)
    lower = jnp.linalg.cholesky(system)
    energy = (local_energy - jnp.mean(local_energy)) / math.sqrt(total)
    column = energy[:, None]
    middle = lax.linalg.triangular_solve(lower, column, left_side=True, lower=True)
    answer = lax.linalg.triangular_solve(
        lower, middle, left_side=True, lower=True, transpose_a=True
    )
    return scale * answer[:, 0]


def body(
    spins,
    local_energy,
    embed_weight,
    position,
    value_weight,
    mixing,
    out_weight,
    up_weight,
    down_weight,
    readout,
):
    samples = spins.shape[0]
    patch_rows = spins.shape[1]
    total = local_energy.shape[0]
    head_count = mixing.shape[0]
    model_width = value_weight.shape[0]
    spin_values = (2 * spins - 1).astype(jnp.float32)
    embedded = jnp.sum(spin_values[..., None] * embed_weight, axis=2) + position.astype(jnp.float32)
    normed = layer_norm(embedded).astype(jnp.bfloat16)
    values = project(normed, value_weight).astype(jnp.bfloat16)
    split_values = values.reshape(samples, patch_rows, head_count, model_width // head_count)
    mixture = jnp.einsum("htu,suhe->sthe", mixing, split_values, preferred_element_type=jnp.float32)
    mixture = mixture.astype(jnp.bfloat16).reshape(samples, patch_rows, model_width)
    residual = embedded + project(mixture, out_weight)
    features = layer_norm(residual).astype(jnp.bfloat16)
    preact = project(features, up_weight)
    hidden = jax.nn.gelu(preact).astype(jnp.bfloat16)
    output = residual + project(hidden, down_weight)
    cotangent = (readout * jnp.tanh(output)).astype(jnp.bfloat16)
    backward = lax.dot_general(
        cotangent, down_weight, (((2,), (1,)), ((), ())), preferred_element_type=jnp.float32
    )
    preact_grad = jax.vjp(jax.nn.gelu, preact)[1](backward)[0].astype(jnp.bfloat16)
    up_block = jnp.einsum("sti,stj->sij", features, preact_grad, preferred_element_type=jnp.float32)
    down_block = jnp.einsum("std,stj->sdj", cotangent, hidden, preferred_element_type=jnp.float32)
    jacobian = jnp.stack([up_block, down_block], axis=1).astype(jnp.bfloat16)
    grouped = lax.all_to_all(jacobian, "param", split_axis=3, concat_axis=0, tiled=True)
    chosen_raw = lax.all_to_all(grouped, "chain", split_axis=2, concat_axis=0, tiled=True)
    centred = center_rows(chosen_raw, total)
    gram = lax.psum(gram_of(centred, total), ("chain", "param"))
    sample_weights = solve_weights(gram, local_energy, total)
    update = -lax.dot_general(
        sample_weights,
        centred,
        (((0,), (0,)), ((), ())),
        precision=lax.Precision.HIGHEST,
        preferred_element_type=jnp.float32,
    )
    return (update[0], update[1].T, sample_weights)


def solution(mesh):
    in_specs = (P(("chain", "param"), None, None), P(), P(), P(), P(), P(), P(), P(), P(), P())
    out_specs = (P("chain", "param"), P("param", "chain"), P())
    return jax.shard_map(body, mesh=mesh, in_specs=in_specs, out_specs=out_specs, check_vma=False)
```

profile of v0, /device:TPU:1, one launch (start us, length us, event | category | flops | bytes accessed | tf_op | source)
XLA Modules:
  0.0 412.8 jit_solution(4878717197872433788)
XLA Ops:
  7.2 0.0 copy-start
  7.2 0.0 copy-start.6
  7.2 0.0 all-reduce.2.cloned.1.call-start
  7.2 0.8 add_convert_fusion
  8.1 1.5 multiply_reduce_fusion
  9.5 0.3 copy.91
  9.9 0.0 copy-start.5
  9.9 1.0 copy.90
  10.9 0.1 add_reduce_fusion
  11.0 0.2 multiply_reduce_fusion.2
  11.2 0.0 copy-done.6
  11.2 0.0 copy-start.4
  11.2 0.4 convolution_convert_fusion
  11.6 0.0 copy-done
  11.6 0.5 fusion.17
  12.1 0.0 copy-done.5
  12.1 0.0 copy-start.9
  12.2 0.0 copy-start.10
  12.2 0.4 fusion.51
  12.5 0.1 multiply_reduce_fusion.1
  12.7 0.0 copy-done.4
  12.7 0.8 fusion.26
  13.4 0.0 copy-start.3
  13.5 1.9 copy-done.3
  15.4 0.0 copy-done.9
  15.4 0.0 copy-done.10
  15.4 2.5 fusion.16
  17.9 6.1 %convert_bitcast_fusion.2 = bf16[4,1,256,1024]{3,2,0,1:T(8,128)(2,1)S(1)} fusion(f32[4,256,1024]{2,1,0:T(8,128)} %copy-done.3, bf16[4,256,256]{1,2,0:T(8,128)(2,1)} %fusion.16, bf16[1024,256]{1,0:T(8,128)(2,1)} %param.18, f32[4,256,256]{1,2,0:T(8,128)S(1)} %get-tuple-element.6, f32[4,256]{1,0:T(4,128)S(1)} %add_rsqrt_fusion, ...), kind=kOutput, calls=%fused_computation.21 | convolution fusion | flops 1096548352 | bytes 8396800 | tf_op jit(solution)/shard_map/sti,stj->sij/dot_general | solution.py:90
  24.0 4.1 convert_bitcast_fusion.1
  28.1 2.3 pad_maximum_fusion
  30.4 7.8 %copy.101 = bf16[4,2,256,1024]{2,0,1,3:T(4,128)(2,1)} copy(bf16[4,2,256,1024]{3,2,0,1:T(8,128)(2,1)} %pad_maximum_fusion) | data formatting | bytes 8388608 | tf_op jit(solution)/shard_map/stack | solution.py:92
  38.2 53.2 %all_to_all.27 = bf16[4,2,256,1024]{2,0,1,3:T(4,128)(2,1)S(1)} all-to-all(bf16[4,2,256,1024]{2,0,1,3:T(4,128)(2,1)} %copy.101), channel_id=1, replica_groups=mesh['chain'=4,'param'=8] {'param'}, dimensions={3} | all-to-all | bytes 8388608 | tf_op jit(solution)/shard_map/all_to_all | solution.py:93
  91.4 2.8 copy.102
  94.2 6.5 %copy.103 = bf16[8,4,2,256,128]{4,3,2,1,0:T(8,128)(2,1)} copy(bf16[8,4,2,256,128]{3,4,0,2,1:T(8,128)(2,1)} %bitcast.90) | data formatting | bytes 8388608 | tf_op jit(solution)/shard_map/all_to_all | solution.py:93
  100.6 6.5 %copy.104 = bf16[32,2,256,128]{3,1,0,2:T(2,128)(2,1)S(1)} copy(bf16[32,2,256,128]{3,2,1,0:T(8,128)(2,1)} %bitcast.91) | data formatting | bytes 8388608 | tf_op jit(solution)/shard_map/all_to_all | solution.py:93
  107.2 96.8 %all_to_all.28 = bf16[32,2,256,128]{3,1,0,2:T(2,128)(2,1)S(1)} all-to-all(bf16[32,2,256,128]{3,1,0,2:T(2,128)(2,1)S(1)} %copy.104), channel_id=1, replica_groups=mesh['chain'=4,'param'=8] {'chain'}, dimensions={2} | all-to-all | bytes 8388608 | tf_op jit(solution)/shard_map/all_to_all | solution.py:94
  203.9 4.9 %copy.105 = bf16[32,2,256,128]{3,2,1,0:T(8,128)(2,1)S(1)} copy(bf16[32,2,256,128]{3,1,0,2:T(2,128)(2,1)S(1)} %all_to_all.28) | data formatting | bytes 8388608 | tf_op jit(solution)/shard_map/all_to_all | solution.py:94
  208.8 0.8 fusion.1
  209.6 5.4 %fusion.2 = f32[4,32,2,64,128]{4,3,0,2,1:T(8,128)S(1)} fusion(f32[2,64,128]{2,1,0:T(8,128)S(1)} %broadcast_multiply_fusion, bf16[32,2,256,128]{3,1,0,2:T(2,128)(2,1)S(1)} %all_to_all.28), kind=kLoop, calls=%fused_computation.3 | loop fusion | flops 6291456 | bytes 12648448 | tf_op jit(solution)/shard_map/div | solution.py:29
  215.0 10.4 %copy.106 = f32[4,32,2,64,128]{4,3,2,1,0:T(8,128)S(1)} copy(f32[4,32,2,64,128]{4,3,0,2,1:T(8,128)S(1)} %fusion.2) | data formatting | bytes 16777216 | tf_op jit(solution)/shard_map/div | solution.py:29
  225.4 0.0 copy-start.2
  225.4 3.2 copy-done.2
  228.7 0.0 copy-start.8
  228.7 17.1 %fusion.18 = f32[128,128]{1,0:T(8,128)} fusion(f32[128,2,64,128]{3,2,1,0:T(8,128)S(1)} %bitcast.88), kind=kOutput, calls=%fused_computation.30 | convolution fusion | flops 3221225472 | bytes 8454144 | tf_op jit(solution)/shard_map/dot_general | solution.py:34
  245.8 0.0 all-reduce.2.cloned.1.call-update
  245.8 0.0 copy-done.8
  245.8 0.6 reduce_sum.80
  247.1 117.5 %all-reduce.2.cloned.1.call-done = f32[128,128]{1,0:T(8,128)} async-done(((f32[128,128]{1,0:T(8,128)}), f32[128,128]{1,0:T(8,128)}) %all-reduce.2.cloned.1.call-update) | async-done | bytes 65552 | tf_op jit(solution)/shard_map/psum | solution.py:96
  364.5 1.5 select_reduce_fusion.1
  367.3 0.9 select_add_fusion
  368.1 0.1 copy.109
  368.2 0.9 fusion.37
  369.1 11.7 %cholesky.13 = f32[128,128]{1,0:T(8,128)S(1)} custom-call(f32[128,128]{1,0:T(8,128)S(1)} %fusion.37), custom_call_target="Cholesky" | custom-call | tf_op jit(solution)/shard_map/jit(cholesky)/cholesky | solution.py:46
  380.8 0.6 compare_reduce_fusion
  381.5 0.7 fusion.34
  382.1 9.8 %custom-call.8 = f32[1,128,128]{1,2,0:T(8,128)S(1)} custom-call(f32[1,128,128]{2,1,0:T(8,128)S(1)} %fusion.34), custom_call_target="InvertDiagBlocksLowerTriangular" | custom-call | tf_op jit(solution)/shard_map/triangular_solve | solution.py:50
  392.0 0.2 convolution_bitcast_fusion.1
  392.1 0.0 copy-start.1
  392.1 0.2 fusion.21
  392.3 0.0 copy-start.7
  392.3 12.5 %fusion.3 = f32[1,2,64,128]{3,0,2,1:T(1,128)S(1)} fusion(f32[128,2,64,128]{3,2,1,0:T(8,128)} %bitcast.89, f32[128]{0:T(128)S(1)} %fusion.21), kind=kOutput, calls=%fused_computation.4 | convolution fusion | flops 25165824 | bytes 8454656 | tf_op jit(solution)/shard_map/dot_general | solution.py:98
  404.9 0.0 copy-done.7
  404.9 0.6 slice_bitcast_fusion
  405.5 0.0 copy-done.1
  (8 shorter events, 0.1 us)
Async XLA Ops:
  7.2 4.4 %copy-start = (bf16[8,256,256]{2,1,0:T(8,128)(2,1)S(1)}, bf16[8,256,256]{2,1,0:T(8,128)(2,1)}, u32[]{:S(2)}) copy-start(bf16[8,256,256]{2,1,0:T(8,128)(2,1)} %param.15) | copy-start | bytes 3145732
  7.2 4.0 copy-start.6
  7.2 357.3 %all-reduce.2.cloned.1.call-start = ((), (), s32[]{:S(2)}) async-start(), calls=%async_computation.2 | async-start | bytes 131072 | tf_op jit(solution)/shard_map/psum | solution.py:96
  9.9 2.3 copy-start.5
  11.2 1.5 copy-start.4
  12.1 3.2 copy-start.9
  12.2 3.2 copy-start.10
  13.4 1.9 copy-start.3
  225.4 3.2 copy-start.2
  228.7 17.1 %copy-start.8 = (f32[128]{0:T(128)S(1)}, f32[128]{0:T(128)}, u32[]{:S(2)}) copy-start(f32[128]{0:T(128)} %param.11) | copy-start | bytes 1540
  392.1 13.4 %copy-start.1 = (bf16[8,256,256]{2,1,0:T(8,128)(2,1)S(1)}, bf16[8,256,256]{2,1,0:T(8,128)(2,1)}, u32[]{:S(2)}) copy-start(bf16[8,256,256]{2,1,0:T(8,128)(2,1)} %param.15) | copy-start | bytes 3145732
  392.3 12.5 %copy-start.7 = (f32[128]{0:T(128)}, f32[128]{0:T(128)S(1)}, u32[]{:S(2)}) copy-start(f32[128]{0:T(128)S(1)} %fusion.21) | copy-start | bytes 1540
Sparse Core Ops, SparseCore 0:
  245.9 118.5 all-reduce.1
where the time goes:
time: 421 us; the launch traced here: 413 us
  blocking collectives  150 us (36%)
  waiting for transfers between devices  117 us (28%)
  local copies, waits for them, and re-layouts  46.1 us (11%)
  matrix products  44.6 us (11%)
  other arithmetic  37.8 us (9%)
  between operations  16.7 us (4%)
    psum x1, waiting for transfers between devices, body(): gram = lax.psum(gram_of(centred, total), ('chain', 'param'))  117 us
    all_to_all x1, blocking collectives, body(): lax.all_to_all(grouped, 'chain', split_axis=2, concat_axis=0, tiled=True)  96.8 us
    all_to_all x1, blocking collectives, body(): lax.all_to_all(jacobian, 'param', split_axis=3, concat_axis=0, tiled=True)  53.2 us
    dot_general x1, matrix products, gram_of(): lax.dot_general(flat, flat, (((1,), (1,)), ((), ())), precision=lax.Preci...  17.1 us
    all_to_all x3, local copies, waits for them, and re-layouts, body(): lax.all_to_all(jacobian, 'param', split_axis=3, concat_axis=0, tiled=True)  15.7 us
    dot_general x1, matrix products, body(): lax.dot_general(sample_weights, centred, (((0,), (0,)), ((), ())), precis...  12.5 us
    another operation x3, other arithmetic, solve_weights(): lower = jnp.linalg.cholesky(system)  12.4 us
    another operation x2, other arithmetic, solve_weights(): lax.linalg.triangular_solve(lower, middle, left_side=True, lower=True, tr...  10.5 us
  transfers between devices with their start and end apart: 1, of which 1 were waited for; matrix products, arithmetic and copies ran while one was open for 0% of the time, Pallas kernels for 0%

commit v1 on v0

v1 whole, which is shorter than its diff:
```python
import functools
import math

import jax
import jax.numpy as jnp
from jax import lax
from jax.experimental import pallas as pl
from jax.experimental.pallas import tpu as pltpu
from jax.sharding import PartitionSpec as P

damping = 0.05
MESH = pl.DeviceIdType.MESH
slope = math.sqrt(2.0 / math.pi)
cubic = 0.044715


def dot(a, b, dims=((1,), (0,))):
    return lax.dot_general(a, b, (dims, ((), ())), preferred_element_type=jnp.float32)


def norm_columns(v):
    width = v.shape[0]
    centred = v - jnp.sum(v, axis=0, keepdims=True) * (1.0 / width)
    spread = jnp.sum(centred * centred, axis=0, keepdims=True) * (1.0 / width)
    return (centred * lax.rsqrt(spread + 1e-05)).astype(jnp.bfloat16)


def greet(count, peer_of):
    barrier = pltpu.get_barrier_semaphore()

    def tell(k, carry):
        pl.semaphore_signal(barrier, inc=1, device_id=peer_of(k), device_id_type=MESH)
        return carry

    lax.fori_loop(1, count, tell, 0)
    pl.semaphore_wait(barrier, count - 1)


def gather_kernel(chips, per_plane, mine, out, send_sem, recv_sem):
    z, p = lax.axis_index("chain"), lax.axis_index("param")
    me = z * per_plane + p // 2

    def peer_of(k):
        q = lax.rem(me + k, chips)
        return (q // per_plane, 2 * lax.rem(q, per_plane) + lax.rem(p, 2))

    greet(chips, peer_of)

    def copy_to(k):
        return pltpu.make_async_remote_copy(
            src_ref=mine,
            dst_ref=out.at[me],
            send_sem=send_sem.at[k],
            recv_sem=recv_sem.at[k],
            device_id=peer_of(k),
            device_id_type=MESH,
        )

    def start(k, carry):
        copy_to(k).start()
        return carry

    def wait(k, carry):
        copy_to(k).wait()
        return carry

    lax.fori_loop(1, chips, start, 0)
    out[me] = mine[...]
    lax.fori_loop(1, chips, wait, 0)


def sum_kernel(count, per_row, parts, out, landed, total, sems):
    z, p = lax.axis_index("chain"), lax.axis_index("param")
    me = z * per_row + p

    def peer_of(k):
        q = lax.rem(me + k, count)
        return (q // per_row, lax.rem(q, per_row))

    greet(count, peer_of)

    def scatter(k):
        return pltpu.make_async_remote_copy(
            src_ref=parts.at[lax.rem(me + k, count)],
            dst_ref=landed.at[me],
            send_sem=sems.at[0, k],
            recv_sem=sems.at[1, k],
            device_id=peer_of(k),
            device_id_type=MESH,
        )

    def spread(k):
        return pltpu.make_async_remote_copy(
            src_ref=total,
            dst_ref=out.at[me],
            send_sem=sems.at[2, k],
            recv_sem=sems.at[3, k],
            device_id=peer_of(k),
            device_id_type=MESH,
        )

    def run(make, verb):
        def step(k, carry):
            getattr(make(k), verb)()
            return carry

        lax.fori_loop(1, count, step, 0)

    run(scatter, "start")
    landed[me] = parts[me]
    run(scatter, "wait")
    total[...] = jnp.sum(landed[...], axis=0)
    run(spread, "start")
    out[me] = total[...]
    run(spread, "wait")


def forward_kernel(
    depth, spins, embed, position, value_t, mixing, out_t, up_t, down_t, down_own, readout, jac, wide
):
    z = lax.axis_index("chain")
    core = lax.rem(lax.axis_index("param"), 2)
    group, heads = embed.shape[0], mixing.shape[0]
    width = value_t.shape[0]
    head_rows = width // heads
    both = down_own.shape[0]
    shard = both // 2
    chunk = min(256, up_t.shape[0])
    chunks = up_t.shape[0] // chunk
    base = position[...].astype(jnp.float32)
    triple = jnp.concatenate([spins[0]] * 3, axis=0)
    embedded = [dot(embed[k], triple) + base for k in range(group)]
    values = [dot(value_t[...], norm_columns(e)).astype(jnp.bfloat16) for e in embedded]
    mixed = []
    for h in range(heads):
        rows = slice(h * head_rows, (h + 1) * head_rows)
        stacked = jnp.concatenate([v[rows] for v in values], axis=0)
        mixed.append(dot(stacked, mixing[h], ((1,), (1,))).astype(jnp.bfloat16))
    slab = pl.ds(pl.multiple_of(z * depth, depth), depth)
    for k in range(group):
        rows = slice(k * head_rows, (k + 1) * head_rows)
        mixture = jnp.concatenate([m[rows] for m in mixed], axis=0)
        residual = embedded[k] + dot(out_t[...], mixture)
        features = norm_columns(residual)
        output = residual
        for c in range(chunks):
            rows = slice(c * chunk, (c + 1) * chunk)
            preact = dot(up_t[rows], features)
            squared = preact * preact
            bend = jnp.tanh(preact * (slope + (slope * cubic) * squared))
            half = 0.5 + 0.5 * bend
            hidden = (preact * half).astype(jnp.bfloat16)
            if c == 0:
                own_hidden = hidden[:both]
                x, s, b = preact[:both], squared[:both], bend[:both]
                rise = half[:both] + (0.5 * x) * (1.0 - b * b) * (slope + (3.0 * slope * cubic) * s)
            output = output + dot(down_t[:, rows], hidden)
        cotangent = (readout[...] * jnp.tanh(output)).astype(jnp.bfloat16)
        grad = (rise * dot(down_own[...], cotangent)).astype(jnp.bfloat16)
        wide[k % 2, 0] = features
        wide[k % 2, 1] = cotangent
        up_block = dot(wide[k % 2, 0, slab, :], grad, ((1,), (1,))).astype(jnp.bfloat16)
        down_block = dot(wide[k % 2, 1, slab, :], own_hidden, ((1,), (1,))).astype(jnp.bfloat16)
        for side in range(2):
            columns = slice(side * shard, (side + 1) * shard)
            where = jnp.bitwise_xor(core, side)
            jac[where, 0, k, :depth, :] = up_block[:, columns]
            jac[where, 0, k, depth:, :] = down_block[:, columns]


def solve_weights(gram, energy, total):
    scale = jnp.trace(gram) / total
    system = gram + damping * scale * jnp.eye(total, dtype=jnp.float32)
    lower = jnp.linalg.cholesky(system)
    column = energy[:, None]
    middle = lax.linalg.triangular_solve(lower, column, left_side=True, lower=True)
    answer = lax.linalg.triangular_solve(
        lower, middle, left_side=True, lower=True, transpose_a=True
    )
    return scale * answer[:, 0]


def body(
    n_chain,
    n_param,
    spins,
    local_energy,
    embed_weight,
    position,
    value_weight,
    mixing,
    out_weight,
    up_weight,
    down_weight,
    readout,
):
    samples, patches, sites = spins.shape
    total = local_energy.shape[0]
    width, hidden_units = up_weight.shape
    heads = mixing.shape[0]
    count = n_chain * n_param
    chips, per_plane = count // 2, n_param // 2
    depth, shard = width // n_chain, hidden_units // n_param
    both = 2 * shard
    vmem = pl.BlockSpec(memory_space=pltpu.VMEM)
    core = lax.axis_index("param") % 2
    offset = (lax.axis_index("param") // 2) * both

    signs = (2 * spins - 1).astype(jnp.bfloat16)
    signs = signs.transpose(0, 2, 1).reshape(samples * sites, patches)
    all_signs = pl.pallas_call(
        functools.partial(gather_kernel, chips, per_plane),
        out_shape=jax.ShapeDtypeStruct((chips, samples * sites, patches), jnp.bfloat16),
        in_specs=[vmem],
        out_specs=vmem,
        scratch_shapes=[pltpu.SemaphoreType.DMA((chips,)), pltpu.SemaphoreType.DMA((chips,))],
        compiler_params=pltpu.CompilerParams(collective_id=0, has_side_effects=True),
    )(signs)

    high = lax.reduce_precision(embed_weight, 8, 7)
    middle = lax.reduce_precision(embed_weight - high, 8, 7)
    low = embed_weight - high - middle
    parts = jnp.stack([high, middle, low]).astype(jnp.bfloat16)
    pick = jnp.eye(samples, dtype=jnp.bfloat16)
    embed = jnp.einsum("kg,acd->kdagc", pick, parts).reshape(samples, width, 3 * samples * sites)

    def turned(weights):
        return lax.dynamic_slice_in_dim(
            jnp.concatenate([weights, weights], axis=0), offset, hidden_units, 0
        )

    down_turned = turned(down_weight)
    whole = lambda *shape: pl.BlockSpec(shape, lambda g: (0,) * len(shape))
    jac = pl.pallas_call(
        functools.partial(forward_kernel, depth),
        grid=(chips,),
        out_shape=jax.ShapeDtypeStruct((2, chips, samples, 2 * depth, shard), jnp.bfloat16),
        in_specs=[
            pl.BlockSpec((1, samples * sites, patches), lambda g: (g, 0, 0)),
            whole(*embed.shape),
            whole(width, patches),
            whole(width, width),
            whole(*mixing.shape),
            whole(width, width),
            whole(hidden_units, width),
            whole(width, hidden_units),
            whole(both, width),
            whole(width, 1),
        ],
        out_specs=pl.BlockSpec((2, 1, samples, 2 * depth, shard), lambda g: (0, g, 0, 0, 0)),
        scratch_shapes=[pltpu.VMEM((2, 2, width, patches), jnp.bfloat16)],
        compiler_params=pltpu.CompilerParams(vmem_limit_bytes=48 * 2**20),
    )(
        all_signs,
        embed,
        position.T,
        value_weight.T,
        mixing,
        out_weight.T,
        turned(up_weight.T),
        down_turned.T,
        down_turned[:both],
        readout[:, None],
    )
    sibling = lax.ppermute(jac[1], "param", [(i, i ^ 1) for i in range(n_param)])
    rows = jnp.stack([jac[0], sibling]).reshape(total, 2 * depth * shard)
    raw = lax.dot_general(
        rows, rows, (((1,), (1,)), ((), ())), preferred_element_type=jnp.float32
    ).reshape(2, total // 2, 2, total // 2)
    raw = jnp.where(core == 1, raw[::-1, :, ::-1], raw)
    raw = pl.pallas_call(
        functools.partial(sum_kernel, count, n_param),
        out_shape=jax.ShapeDtypeStruct((count, samples, total), jnp.float32),
        in_specs=[vmem],
        out_specs=vmem,
        scratch_shapes=[
            pltpu.VMEM((count, samples, total), jnp.float32),
            pltpu.VMEM((samples, total), jnp.float32),
            pltpu.SemaphoreType.DMA((4, count)),
        ],
        compiler_params=pltpu.CompilerParams(collective_id=1, has_side_effects=True),
    )(raw.reshape(count, samples, total)).reshape(total, total)
    average = jnp.mean(raw, axis=0)
    gram = (raw - average[None, :] - average[:, None] + jnp.mean(average)) / total
    energy = (local_energy - jnp.mean(local_energy)) / math.sqrt(total)
    energy = energy.reshape(chips, 2, samples).swapaxes(0, 1).reshape(total)
    solved = solve_weights(gram, energy, total)
    sample_weights = solved.reshape(2, chips, samples).swapaxes(0, 1).reshape(total)
    pull = ((solved - jnp.mean(solved)) * (-1.0 / math.sqrt(total))).reshape(2, total // 2)
    pull = jnp.where(core == 1, pull[::-1], pull).reshape(total)
    update = jnp.sum(pull[:, None] * rows.astype(jnp.float32), axis=0).reshape(2, depth, shard)
    return (update[0], update[1].T, sample_weights)


def solution(mesh):
    in_specs = (P(("chain", "param"), None, None), P(), P(), P(), P(), P(), P(), P(), P(), P())
    out_specs = (P("chain", "param"), P("param", "chain"), P())
    run = functools.partial(body, mesh.shape["chain"], mesh.shape["param"])
    return jax.shard_map(run, mesh=mesh, in_specs=in_specs, out_specs=out_specs, check_vma=False)
```

time: 421 us -> 188 us (0.45); the launches traced: 413 us -> 187 us
  blocking collectives: 150 us -> 0 us
  Pallas kernels: 0 us -> 118 us
  waiting for transfers between devices: 117 us -> 0.01 us
  matrix products: 44.6 us -> 6.82 us
  local copies, waits for them, and re-layouts: 46.1 us -> 23.2 us
  between operations: 16.7 us -> 4.29 us
  other arithmetic: 37.8 us -> 33.3 us
    all_to_all x2 -> x0, blocking collectives: 150 us -> none  [the longest x1 96.8 us: body(): lax.all_to_all(grouped, 'chain', split_axis=2, concat_axis=0, tiled=True)]
    pallas_call x0 -> x3, Pallas kernels: none -> 118 us  [the longest x1 91 us: body(): pl.pallas_call(functools.partial(forward_kernel, depth), grid=(chips,), o...]
    psum x1 -> x0, waiting for transfers between devices: 117 us -> none  [body(): gram = lax.psum(gram_of(centred, total), ('chain', 'param'))]
    dot_general x9 -> x1, matrix products: 44.3 us -> 5.83 us  [body(): lax.dot_general(rows, rows, (((1,), (1,)), ((), ())), preferred_element_t...]
    all_to_all x4 -> x0, local copies, waits for them, and re-layouts: 20.6 us -> none  [the longest x3 15.7 us: body(): lax.all_to_all(jacobian, 'param', split_axis=3, concat_axis=0, tiled=True)]
    div x1, local copies, waits for them, and re-layouts: 10.4 us -> 0.09 us  [body(): average = jnp.mean(raw, axis=0)]
    div x4 -> x2, other arithmetic: 5.43 us -> 0.61 us  [the longest x1 0.6 us: body(): average = jnp.mean(raw, axis=0)]
    another operation x1 -> x5, local copies, waits for them, and re-layouts: 7.85 us -> 9.69 us  [the longest x3 9.55 us: body(): rows = jnp.stack([jac[0], sibling]).reshape(total, 2 * depth * shard)]
  transfers between devices with their start and end apart: 1 -> 1, of which waited for: 1 -> 0; matrix products, arithmetic and copies ran while one was open for 0% -> 3% of each run, Pallas kernels for 0% -> 0%
where the time goes in v1:
time: 188 us; the launch traced here: 187 us
  Pallas kernels  118 us (63%)
  other arithmetic  33.3 us (18%)
  local copies, waits for them, and re-layouts  23.2 us (12%)
  matrix products  6.82 us (4%)
  between operations  4.29 us (2%)
    pallas_call x1, Pallas kernels, body(): pl.pallas_call(functools.partial(forward_kernel, depth), grid=(chips,), o...  91 us
    pallas_call x1, Pallas kernels, body(): pl.pallas_call(functools.partial(sum_kernel, count, n_param), out_shape=j...  17.1 us
    another operation x3, other arithmetic, solve_weights(): lower = jnp.linalg.cholesky(system)  12.4 us
    another operation x2, other arithmetic, solve_weights(): lax.linalg.triangular_solve(lower, middle, left_side=True, lower=True, tr...  10.5 us
    pallas_call x1, Pallas kernels, body(): pl.pallas_call(functools.partial(gather_kernel, chips, per_plane), out_sh...  10 us
    another operation x3, local copies, waits for them, and re-layouts, body(): rows = jnp.stack([jac[0], sibling]).reshape(total, 2 * depth * shard)  9.55 us
    dot_general x1, matrix products, body(): lax.dot_general(rows, rows, (((1,), (1,)), ((), ())), preferred_element_t...  5.83 us
    unnamed x23, local copies, waits for them, and re-layouts  5.69 us
  transfers between devices with their start and end apart: 1, of which 0 were waited for; matrix products, arithmetic and copies ran while one was open for 3% of the time, Pallas kernels for 0%

profile of v1, /device:TPU:1, one launch (start us, length us, event | category | flops | bytes accessed | tf_op | source)
XLA Modules:
  0.0 187.5 jit_solution(8239668368118936761)
XLA Ops:
  0.6 0.0 copy-start.6
  0.6 0.0 copy-start.5
  0.7 0.0 copy-start.2
  0.7 0.0 copy-start.3
  0.7 0.0 copy-start.4
  0.7 0.0 copy-start.7
  0.7 0.0 copy-start
  0.7 1.4 copy.26
  2.1 2.6 %fusion.3 = (bf16[1024,256]{1,0:T(8,128)(2,1)S(1)}, bf16[1024,256]{1,0:T(8,128)(2,1)S(1)}) fusion(s32[]{:T(128)S(6)} %select_n.45, bf16[1024,256]{1,0:T(8,128)(2,1)} %param.18, bf16[1024,256]{1,0:T(8,128)(2,1)S(1)} %bitcast.60), kind=kLoop, calls=%fused_computation.11 | loop fusion | flops 2097152 | bytes 2097156 | tf_op jit(solution)/shard_map/concatenate | solution.py:229
  4.7 0.2 copy.28.down_t
  4.9 0.0 copy-done.6
  5.0 0.1 broadcast_multiply_fusion
  5.1 0.2 copy.27.embed
  5.3 0.0 copy-done.5
  5.3 0.6 reshape.106.mine
  5.9 10.0 %shard_map.121.spins = bf16[16,16,256]{2,1,0:T(8,128)(2,1)} custom-call(bf16[16,256]{1,0:T(8,128)(2,1)} %reshape.106.mine), custom_call_target="tpu_custom_call" | custom-call | tf_op jit(solution)/shard_map/pallas_call | solution.py:211
  16.0 0.0 copy-done.2
  16.0 0.1 copy.23
  16.1 0.0 copy-done.3
  16.1 0.1 copy.24
  16.2 0.0 copy-done.4
  16.2 0.1 copy.25
  16.3 0.0 copy-done.7
  16.3 0.1 copy.29.readout
  16.5 0.0 copy-done
  16.5 0.0 copy-start.1
  16.5 0.9 copy-done.1
  17.4 91.0 %shard_map.122 = bf16[2,16,4,128,128]{4,3,2,1,0:T(8,128)(2,1)} custom-call(bf16[16,16,256]{2,1,0:T(8,128)(2,1)S(1)} %copy-done.1, bf16[4,256,48]{2,1,0:T(8,128)(2,1)S(1)} %copy.27.embed, bf16[256,256]{1,0:T(8,128)(2,1)S(1)} %bitcast.56, bf16[256,256]{1,0:T(8,128)(2,1)S(1)} %bitcast.57, bf16[8,256,256]{2,1,0:T(8,128)(2,1)S(1)} %copy-done, ...), custom_call_target="tpu_custom_call" | custom-call | tf_op jit(solution)/shard_map/pallas_call | solution.py:234
  108.4 4.0 %fusion.17 = (bf16[1,16,4,128,128]{4,3,2,1,0:T(8,128)(2,1)S(1)}, bf16[16,4,128,128]{3,2,1,0:T(8,128)(2,1)}) fusion(bf16[2,16,4,128,128]{4,3,2,1,0:T(8,128)(2,1)} %shard_map.122), kind=kLoop, calls=%fused_computation.51 | loop fusion | bytes 8388608 | tf_op jit(solution)/shard_map/slice | solution.py:266
  112.4 0.0 copy-start.8
  112.4 1.6 collective-permute-start
  114.0 2.3 %stack.32 = bf16[1,64,16384]{2,1,0:T(8,128)(2,1)} reshape(bf16[1,16,4,128,128]{4,3,2,1,0:T(8,128)(2,1)S(1)} %get-tuple-element.5) | data formatting | bytes 4194304 | tf_op jit(solution)/shard_map/stack | solution.py:266
  116.4 0.0 copy-done.8
  116.4 0.6 reduce_sum.58
  117.7 0.1 reshape.110
  117.8 0.1 reshape.114
  117.9 3.1 %constant_dynamic-update-slice_fusion.1 = bf16[2,64,16384]{2,1,0:T(8,128)(2,1)} fusion(bf16[1,64,16384]{2,1,0:T(8,128)(2,1)} %stack.32), kind=kLoop, calls=%fused_computation.33 | loop fusion | bytes 4194304
  121.0 0.0 collective-permute-done
  121.0 4.2 %stack.33 = bf16[1,64,16384]{2,1,0:T(8,128)(2,1)} reshape(bf16[16,4,128,128]{3,2,1,0:T(8,128)(2,1)} %collective-permute-done) | data formatting | bytes 4194304 | tf_op jit(solution)/shard_map/stack | solution.py:266
  125.2 3.0 %constant_dynamic-update-slice_fusion = bf16[2,64,16384]{2,1,0:T(8,128)(2,1)} fusion(bf16[2,64,16384]{2,1,0:T(8,128)(2,1)} %constant_dynamic-update-slice_fusion.1, bf16[1,64,16384]{2,1,0:T(8,128)(2,1)} %stack.33), kind=kLoop, calls=%fused_computation.32 | loop fusion | bytes 4194304 | tf_op jit(solution)/shard_map/stack | solution.py:266
  128.2 5.8 %fusion = f32[2,64,2,64]{3,1,2,0:T(8,128)S(1)} fusion(bf16[2,64,16384]{2,1,0:T(8,128)(2,1)} %constant_dynamic-update-slice_fusion), kind=kOutput, calls=%fused_computation.1 | convolution fusion | flops 536870912 | bytes 4259840 | tf_op jit(solution)/shard_map/dot_general | solution.py:267
  134.1 0.1 copy.30
  134.2 0.8 reshape.108.parts
  134.9 17.1 %shard_map.123 = f32[32,4,128]{2,1,0:T(4,128)} custom-call(f32[32,4,128]{2,1,0:T(4,128)} %reshape.108.parts), custom_call_target="tpu_custom_call" | custom-call | tf_op jit(solution)/shard_map/pallas_call | solution.py:271
  152.1 0.9 reduce_sum.55
  153.0 0.6 broadcast_multiply_fusion.2
  153.6 0.1 div.57
  154.3 1.6 select_reduce_fusion.1
  157.2 0.9 select_add_fusion
  158.1 0.1 copy.31
  158.2 0.9 fusion.8
  159.2 11.7 %cholesky.16 = f32[128,128]{1,0:T(8,128)S(1)} custom-call(f32[128,128]{1,0:T(8,128)S(1)} %fusion.8), custom_call_target="Cholesky" | custom-call | tf_op jit(solution)/shard_map/jit(cholesky)/cholesky | solution.py:174
  170.9 0.6 compare_reduce_fusion
  171.6 0.7 fusion.5
  172.2 9.8 %custom-call.8 = f32[1,128,128]{1,2,0:T(8,128)S(1)} custom-call(f32[1,128,128]{2,1,0:T(8,128)S(1)} %fusion.5), custom_call_target="InvertDiagBlocksLowerTriangular" | custom-call | tf_op jit(solution)/shard_map/triangular_solve | solution.py:177
  182.0 0.2 convolution_bitcast_fusion.1
  182.2 0.8 fusion.16
  183.0 0.1 squeeze.9
  183.8 0.1 mul.59
  183.9 2.2 %multiply_reduce_fusion = f32[128,128]{1,0:T(8,128)S(1)} fusion(bf16[1,16,4,128,128]{4,3,2,1,0:T(8,128)(2,1)} %bitcast.23, bf16[1,16,4,128,128]{4,3,2,1,0:T(8,128)(2,1)S(1)} %get-tuple-element.5, f32[2,16,4]{2,1,0:T(8,128)S(1)} %mul.59), kind=kLoop, calls=%fused_computation | loop fusion | flops 8372224 | bytes 4260352 | tf_op jit(solution)/shard_map/reduce_sum | solution.py:291
  186.1 0.6 slice_bitcast_fusion.1
  186.7 0.1 mul.62
  186.8 0.6 reshape.112
  (13 shorter events, 0.2 us)
Async XLA Ops:
  0.6 4.3 %copy-start.6 = (f32[4,256]{1,0:T(4,128)S(1)}, f32[4,256]{1,0:T(4,128)}, u32[]{:S(2)}) copy-start(f32[4,256]{1,0:T(4,128)} %param.12) | copy-start | bytes 12292
  0.6 4.7 %copy-start.5 = (s32[4,256,4]{1,2,0:T(4,128)S(1)}, s32[4,256,4]{1,2,0:T(4,128)}, u32[]{:S(2)}) copy-start(s32[4,256,4]{1,2,0:T(4,128)} %param.10) | copy-start | bytes 49156
  0.7 15.3 %copy-start.2 = (bf16[256,256]{1,0:T(8,128)(2,1)S(1)}, bf16[256,256]{1,0:T(8,128)(2,1)}, u32[]{:S(2)}) copy-start(bf16[256,256]{1,0:T(8,128)(2,1)} %param.13) | copy-start | bytes 393220
  0.7 15.4 %copy-start.3 = (bf16[256,256]{1,0:T(8,128)(2,1)S(1)}, bf16[256,256]{1,0:T(8,128)(2,1)}, u32[]{:S(2)}) copy-start(bf16[256,256]{1,0:T(8,128)(2,1)} %param.14) | copy-start | bytes 393220
  0.7 15.5 %copy-start.4 = (bf16[256,256]{1,0:T(8,128)(2,1)S(1)}, bf16[256,256]{1,0:T(8,128)(2,1)}, u32[]{:S(2)}) copy-start(bf16[256,256]{1,0:T(8,128)(2,1)} %param.16) | copy-start | bytes 393220
  0.7 15.6 %copy-start.7 = (f32[256]{0:T(256)S(1)}, f32[256]{0:T(256)}, u32[]{:S(2)}) copy-start(f32[256]{0:T(256)} %param.19) | copy-start | bytes 3076
  0.7 15.8 %copy-start = (bf16[8,256,256]{2,1,0:T(8,128)(2,1)S(1)}, bf16[8,256,256]{2,1,0:T(8,128)(2,1)}, u32[]{:S(2)}) copy-start(bf16[8,256,256]{2,1,0:T(8,128)(2,1)} %mixing.1) | copy-start | bytes 3145732
  16.5 0.9 copy-start.1
  112.4 4.0 %copy-start.8 = (f32[128]{0:T(128)S(1)}, f32[128]{0:T(128)}, u32[]{:S(2)}) copy-start(f32[128]{0:T(128)} %param.11) | copy-start | bytes 1540
  112.4 8.6 %collective-permute-start = (bf16[16,4,128,128]{3,2,1,0:T(8,128)(2,1)}, bf16[16,4,128,128]{3,2,1,0:T(8,128)(2,1)}, u32[]{:S(2)}, u32[]{:S(2)}) collective-permute-start(bf16[16,4,128,128]{3,2,1,0:T(8,128)(2,1)} %get-tuple-element.6), channel_id=1, source_target_pairs={{0,1},{1,0},{2,3},{3,2},{4,5},{5,4},{6,7},{7,6},{8,9},{9,8},{10,11... | collective-permute-start | bytes 6291464 | tf_op jit(solution)/shard_map/ppermute | solution.py:265

commit v2 on v1

v2 whole, which is shorter than its diff:
```python
import functools
import math

import jax
import jax.numpy as jnp
from jax import lax
from jax.experimental import pallas as pl
from jax.experimental.pallas import tpu as pltpu
from jax.sharding import PartitionSpec as P

damping = 0.05
MESH = pl.DeviceIdType.MESH
slope = math.sqrt(2.0 / math.pi)
cubic = 0.044715


def dot(a, b, dims=((1,), (0,))):
    return lax.dot_general(a, b, (dims, ((), ())), preferred_element_type=jnp.float32)


def norm_columns(v):
    width = v.shape[0]
    centred = v - jnp.sum(v, axis=0, keepdims=True) * (1.0 / width)
    spread = jnp.sum(centred * centred, axis=0, keepdims=True) * (1.0 / width)
    return (centred * lax.rsqrt(spread + 1e-05)).astype(jnp.bfloat16)


def greet(count, peer_of):
    barrier = pltpu.get_barrier_semaphore()

    def tell(k, carry):
        pl.semaphore_signal(barrier, inc=1, device_id=peer_of(k), device_id_type=MESH)
        return carry

    lax.fori_loop(1, count, tell, 0)
    pl.semaphore_wait(barrier, count - 1)


def sum_kernel(count, per_row, parts, out, landed, total, sems):
    z, p = lax.axis_index("chain"), lax.axis_index("param")
    me = z * per_row + p

    def peer_of(k):
        q = lax.rem(me + k, count)
        return (q // per_row, lax.rem(q, per_row))

    greet(count, peer_of)

    def scatter(k):
        return pltpu.make_async_remote_copy(
            src_ref=parts.at[lax.rem(me + k, count)],
            dst_ref=landed.at[me],
            send_sem=sems.at[0, k],
            recv_sem=sems.at[1, k],
            device_id=peer_of(k),
            device_id_type=MESH,
        )

    def spread(k):
        return pltpu.make_async_remote_copy(
            src_ref=total,
            dst_ref=out.at[me],
            send_sem=sems.at[2, k],
            recv_sem=sems.at[3, k],
            device_id=peer_of(k),
            device_id_type=MESH,
        )

    def run(make, verb):
        def step(k, carry):
            getattr(make(k), verb)()
            return carry

        lax.fori_loop(1, count, step, 0)

    run(scatter, "start")
    landed[me] = parts[me]
    run(scatter, "wait")
    total[...] = jnp.sum(landed[...], axis=0)
    run(spread, "start")
    out[me] = total[...]
    run(spread, "wait")


def forward_kernel(
    n_chain,
    n_param,
    mine,
    embed,
    position,
    value_t,
    mixing,
    out_t,
    up_t,
    down_t,
    down,
    readout,
    jac,
    spins,
    stage,
    wide,
    spin_sems,
    send_sem,
    recv_sem,
):
    z, p = lax.axis_index("chain"), lax.axis_index("param")
    group, heads = embed.shape[0], mixing.shape[0]
    width, hidden_units = down_t.shape
    head_rows, depth, shard = width // heads, width // n_chain, hidden_units // n_param
    chunk = min(256, hidden_units)
    chunks = hidden_units // chunk

    barrier = pltpu.get_barrier_semaphore()

    def tell_chain(k, carry):
        there = (lax.rem(z + n_chain - k, n_chain), p)
        pl.semaphore_signal(barrier, inc=1, device_id=there, device_id_type=MESH)
        return carry

    def tell_plane(m, carry):
        there = (z, lax.rem(p + m, n_param))
        pl.semaphore_signal(barrier, inc=1, device_id=there, device_id_type=MESH)
        return carry

    lax.fori_loop(1, n_chain, tell_chain, 0)
    lax.fori_loop(1, n_param, tell_plane, 0)
    pl.semaphore_wait(barrier, n_chain + n_param - 2)

    def spin_copy(k):
        return pltpu.make_async_remote_copy(
            src_ref=mine,
            dst_ref=spins.at[z],
            send_sem=spin_sems.at[0, k],
            recv_sem=spin_sems.at[1, k],
            device_id=(lax.rem(z + n_chain - k, n_chain), p),
            device_id_type=MESH,
        )

    def slice_copy(g, k, m):
        owner = lax.rem(p + m, n_param)
        return pltpu.make_async_remote_copy(
            src_ref=stage.at[g, k, owner],
            dst_ref=jac.at[p, g, k],
            send_sem=send_sem.at[g, k, m],
            recv_sem=recv_sem.at[g, k, m],
            device_id=(z, owner),
            device_id_type=MESH,
        )

    def start_spins(k, carry):
        spin_copy(k).start()
        return carry

    lax.fori_loop(1, n_chain, start_spins, 0)
    spins[z] = mine[...]
    slab = pl.ds(pl.multiple_of(z * depth, depth), depth)

    def one_group(step, carry):
        @pl.when(step > 0)
        def _():
            spin_copy(step).wait_recv()

        g = lax.rem(z + step, n_chain)
        base = position[...].astype(jnp.float32)
        triple = jnp.concatenate([spins[g]] * 3, axis=0)
        embedded = [dot(embed[k], triple) + base for k in range(group)]
        values = [dot(value_t[...], norm_columns(e)).astype(jnp.bfloat16) for e in embedded]
        mixed = []
        for h in range(heads):
            rows = slice(h * head_rows, (h + 1) * head_rows)
            stacked = jnp.concatenate([v[rows] for v in values], axis=0)
            mixed.append(dot(stacked, mixing[h], ((1,), (1,))).astype(jnp.bfloat16))
        for k in range(group):
            rows = slice(k * head_rows, (k + 1) * head_rows)
            mixture = jnp.concatenate([m[rows] for m in mixed], axis=0)
            residual = embedded[k] + dot(out_t[...], mixture)
            features = norm_columns(residual)
            output = residual
            units, rises = [], []
            for c in range(chunks):
                rows = slice(c * chunk, (c + 1) * chunk)
                preact = dot(up_t[rows], features)
                squared = preact * preact
                bend = jnp.tanh(preact * (slope + (slope * cubic) * squared))
                half = 0.5 + 0.5 * bend
                hidden = (preact * half).astype(jnp.bfloat16)
                units.append(hidden)
                rises.append(
                    half
                    + (0.5 * preact)
                    * (1.0 - bend * bend)
                    * (slope + (3.0 * slope * cubic) * squared)
                )
                output = output + dot(down_t[:, rows], hidden)
            cotangent = (readout[...] * jnp.tanh(output)).astype(jnp.bfloat16)
            wide[k % 2, 0] = features
            wide[k % 2, 1] = cotangent
            left, right = wide[k % 2, 0, slab, :], wide[k % 2, 1, slab, :]
            for c in range(chunks):
                rows = slice(c * chunk, (c + 1) * chunk)
                grad = (rises[c] * dot(down[rows], cotangent)).astype(jnp.bfloat16)
                up_block = dot(left, grad, ((1,), (1,))).astype(jnp.bfloat16)
                down_block = dot(right, units[c], ((1,), (1,))).astype(jnp.bfloat16)
                for part in range(chunk // shard):
                    columns = slice(part * shard, (part + 1) * shard)
                    owner = c * (chunk // shard) + part
                    stage[g, k, owner, :depth, :] = up_block[:, columns]
                    stage[g, k, owner, depth:, :] = down_block[:, columns]

            def start_slices(m, carry):
                slice_copy(g, k, m).start()
                return carry

            lax.fori_loop(1, n_param, start_slices, 0)
            jac[p, g, k] = stage[g, k, p]
        return carry

    lax.fori_loop(0, n_chain, one_group, 0)

    def end_spins(k, carry):
        spin_copy(k).wait_send()
        return carry

    lax.fori_loop(1, n_chain, end_spins, 0)

    def end_slices(i, carry):
        m = 1 + lax.rem(i, n_param - 1)
        gk = i // (n_param - 1)
        slice_copy(gk // group, lax.rem(gk, group), m).wait()
        return carry

    lax.fori_loop(0, n_chain * group * (n_param - 1), end_slices, 0)


def solve_weights(gram, energy, total):
    scale = jnp.trace(gram) / total
    system = gram + damping * scale * jnp.eye(total, dtype=jnp.float32)
    lower = jnp.linalg.cholesky(system)
    column = energy[:, None]
    middle = lax.linalg.triangular_solve(lower, column, left_side=True, lower=True)
    answer = lax.linalg.triangular_solve(
        lower, middle, left_side=True, lower=True, transpose_a=True
    )
    return scale * answer[:, 0]


def body(
    n_chain,
    n_param,
    spins,
    local_energy,
    embed_weight,
    position,
    value_weight,
    mixing,
    out_weight,
    up_weight,
    down_weight,
    readout,
):
    samples, patches, sites = spins.shape
    total = local_energy.shape[0]
    width, hidden_units = up_weight.shape
    heads = mixing.shape[0]
    count = n_chain * n_param
    depth, shard = width // n_chain, hidden_units // n_param
    vmem = pl.BlockSpec(memory_space=pltpu.VMEM)

    signs = (2 * spins - 1).astype(jnp.bfloat16)
    signs = signs.transpose(0, 2, 1).reshape(samples * sites, patches)
    high = lax.reduce_precision(embed_weight, 8, 7)
    middle = lax.reduce_precision(embed_weight - high, 8, 7)
    low = embed_weight - high - middle
    parts = jnp.stack([high, middle, low]).astype(jnp.bfloat16)
    pick = jnp.eye(samples, dtype=jnp.bfloat16)
    embed = jnp.einsum("kg,acd->kdagc", pick, parts).reshape(samples, width, 3 * samples * sites)

    sems = (n_chain, samples, n_param)
    jac = pl.pallas_call(
        functools.partial(forward_kernel, n_chain, n_param),
        out_shape=jax.ShapeDtypeStruct(
            (n_param, n_chain, samples, 2 * depth, shard), jnp.bfloat16
        ),
        in_specs=[vmem] * 10,
        out_specs=vmem,
        scratch_shapes=[
            pltpu.VMEM((n_chain, samples * sites, patches), jnp.bfloat16),
            pltpu.VMEM((n_chain, samples, n_param, 2 * depth, shard), jnp.bfloat16),
            pltpu.VMEM((2, 2, width, patches), jnp.bfloat16),
            pltpu.SemaphoreType.DMA((2, n_chain)),
            pltpu.SemaphoreType.DMA(sems),
            pltpu.SemaphoreType.DMA(sems),
        ],
        compiler_params=pltpu.CompilerParams(
            collective_id=0, has_side_effects=True, vmem_limit_bytes=56 * 2**20
        ),
    )(
        signs,
        embed,
        position.T,
        value_weight.T,
        mixing,
        out_weight.T,
        up_weight.T,
        down_weight.T,
        down_weight,
        readout[:, None],
    )
    rows = jac.reshape(total, 2 * depth * shard)
    raw = lax.dot_general(
        rows, rows, (((1,), (1,)), ((), ())), preferred_element_type=jnp.float32
    )
    raw = pl.pallas_call(
        functools.partial(sum_kernel, count, n_param),
        out_shape=jax.ShapeDtypeStruct((count, samples, total), jnp.float32),
        in_specs=[vmem],
        out_specs=vmem,
        scratch_shapes=[
            pltpu.VMEM((count, samples, total), jnp.float32),
            pltpu.VMEM((samples, total), jnp.float32),
            pltpu.SemaphoreType.DMA((4, count)),
        ],
        compiler_params=pltpu.CompilerParams(collective_id=1, has_side_effects=True),
    )(raw.reshape(count, samples, total)).reshape(total, total)
    average = jnp.mean(raw, axis=0)
    gram = (raw - average[None, :] - average[:, None] + jnp.mean(average)) / total
    energy = (local_energy - jnp.mean(local_energy)) / math.sqrt(total)
    energy = energy.reshape(n_chain, n_param, samples).swapaxes(0, 1).reshape(total)
    solved = solve_weights(gram, energy, total)
    sample_weights = solved.reshape(n_param, n_chain, samples).swapaxes(0, 1).reshape(total)
    pull = (solved - jnp.mean(solved)) * (-1.0 / math.sqrt(total))
    update = jnp.sum(pull[:, None] * rows.astype(jnp.float32), axis=0).reshape(2, depth, shard)
    return (update[0], update[1].T, sample_weights)


def solution(mesh):
    in_specs = (P(("chain", "param"), None, None), P(), P(), P(), P(), P(), P(), P(), P(), P())
    out_specs = (P("chain", "param"), P("param", "chain"), P())
    run = functools.partial(body, mesh.shape["chain"], mesh.shape["param"])
    return jax.shard_map(run, mesh=mesh, in_specs=in_specs, out_specs=out_specs, check_vma=False)
```

time: 188 us -> 152 us (0.81)
  Pallas kernels: 118 us -> 77 us
  local copies, waits for them, and re-layouts: 23.2 us -> 29 us
    pallas_call x2 -> x1, Pallas kernels: 101 us -> 60.7 us  [body(): pl.pallas_call(functools.partial(forward_kernel, n_chain, n_param), out_s...]
    another operation x5 -> x1, local copies, waits for them, and re-layouts: 9.69 us -> 0.11 us  [the longest x3 9.55 us: body(): rows = jnp.stack([jac[0], sibling]).reshape(total, 2 * depth * shard)]
    dot_general x0 -> x2, local copies, waits for them, and re-layouts: none -> 7.75 us  [body(): lax.dot_general(rows, rows, (((1,), (1,)), ((), ())), preferred_element_t...]
    reshape x3, local copies, waits for them, and re-layouts: 1.5 us -> 8.02 us  [the longest x1 7.31 us: body(): rows = jac.reshape(total, 2 * depth * shard)]
    slice x2 -> x0, local copies, waits for them, and re-layouts: 4.03 us -> none  [the longest x1 4.02 us: body(): rows = jnp.stack([jac[0], sibling]).reshape(total, 2 * depth * shard)]
    unnamed x23 -> x7, local copies, waits for them, and re-layouts: 5.69 us -> 9.1 us
    concatenate x1 -> x0, other arithmetic: 2.57 us -> none  [turned(): jnp.concatenate([weights, weights], axis=0)]
  transfers between devices with their start and end apart: 1 -> 0, of which waited for: 0 -> 0; matrix products, arithmetic and copies ran while one was open for 3% -> 0% of each run, Pallas kernels for 0% -> 0%
where the time goes in v2:
time: 152 us; the launch traced here: 151 us
  Pallas kernels  77 us (51%)
  other arithmetic  33 us (22%)
  local copies, waits for them, and re-layouts  29 us (19%)
  matrix products  7.75 us (5%)
  between operations  4.08 us (3%)
    pallas_call x1, Pallas kernels, body(): pl.pallas_call(functools.partial(forward_kernel, n_chain, n_param), out_s...  60.7 us
    pallas_call x1, Pallas kernels, body(): pl.pallas_call(functools.partial(sum_kernel, count, n_param), out_shape=j...  16.3 us
    another operation x3, other arithmetic, solve_weights(): lower = jnp.linalg.cholesky(system)  12.4 us
    another operation x2, other arithmetic, solve_weights(): lax.linalg.triangular_solve(lower, middle, left_side=True, lower=True, tr...  10.5 us
    unnamed x7, local copies, waits for them, and re-layouts  9.1 us
    dot_general x2, local copies, waits for them, and re-layouts, body(): lax.dot_general(rows, rows, (((1,), (1,)), ((), ())), preferred_element_t...  7.75 us
    reshape x1, local copies, waits for them, and re-layouts, body(): rows = jac.reshape(total, 2 * depth * shard)  7.31 us
    dot_general x1, matrix products, body(): lax.dot_general(rows, rows, (((1,), (1,)), ((), ())), preferred_element_t...  6.77 us

profile of v2, /device:TPU:1, one launch (start us, length us, event | category | flops | bytes accessed | tf_op | source)
XLA Modules:
  0.0 150.8 jit_solution(8300086903367719289)
XLA Ops:
  0.6 0.7 fusion.10
  1.4 0.1 broadcast_multiply_fusion
  1.5 0.9 copy.29.embed
  2.3 2.1 %copy.28 = bf16[1024,256]{0,1:T(8,128)(2,1)} copy(bf16[1024,256]{1,0:T(8,128)(2,1)} %down.1) | data formatting | bytes 1048576 | tf_op args[8]
  4.4 2.0 %copy.27 = bf16[256,1024]{0,1:T(8,128)(2,1)} copy(bf16[256,1024]{1,0:T(8,128)(2,1)} %param.17) | data formatting | bytes 1048576 | tf_op args[7]
  6.4 1.7 %copy.24 = bf16[256,256]{0,1:T(8,128)(2,1)} copy(bf16[256,256]{1,0:T(8,128)(2,1)} %param.13) | data formatting | bytes 262144 | tf_op args[3]
  8.1 1.7 %copy.25 = bf16[256,256]{0,1:T(8,128)(2,1)} copy(bf16[256,256]{1,0:T(8,128)(2,1)} %param.14) | data formatting | bytes 262144 | tf_op args[4]
  9.8 1.7 %copy.26 = bf16[256,256]{0,1:T(8,128)(2,1)} copy(bf16[256,256]{1,0:T(8,128)(2,1)} %param.16) | data formatting | bytes 262144 | tf_op args[6]
  11.4 1.5 copy.30.readout
  12.9 0.7 fusion.7
  13.6 0.6 reshape.102.mine
  14.2 60.7 %shard_map.121 = bf16[8,4,4,128,128]{4,3,2,1,0:T(8,128)(2,1)} custom-call(bf16[16,256]{1,0:T(8,128)(2,1)} %reshape.102.mine, bf16[4,256,48]{2,1,0:T(8,128)(2,1)} %copy.29.embed, bf16[256,256]{1,0:T(8,128)(2,1)} %bitcast.53, bf16[256,256]{1,0:T(8,128)(2,1)} %bitcast.54, bf16[8,256,256]{2,1,0:T(8,128)(2,1)} %mixing.1, bf16[256,256]{1,0:T(8,128)(2,1)} %bitcast.55, ...), custom_call_target="tpu_custom_call" | custom-call | tf_op jit(solution)/shard_map/pallas_call | solution.py:279
  74.9 7.1 %dot_general.15 = bf16[32,4,16384]{2,1,0:T(4,128)(2,1)} reshape(bf16[8,4,4,128,128]{4,3,2,1,0:T(8,128)(2,1)} %shard_map.121) | data formatting | bytes 8388608 | tf_op jit(solution)/shard_map/dot_general | solution.py:310
  82.0 7.3 %reshape.109 = bf16[128,16384,1]{1,0,2:T(8,128)(2,1)} reshape(bf16[8,4,4,128,128]{4,3,2,1,0:T(8,128)(2,1)} %shard_map.121) | data formatting | bytes 8388608 | tf_op jit(solution)/shard_map/reshape | solution.py:309
  89.3 0.0 copy-start
  89.3 6.8 %fusion = f32[32,4,128]{2,0,1:T(8,128)S(1)} fusion(bf16[128,16384,1]{1,0,2:T(8,128)(2,1)} %reshape.109, bf16[32,4,16384]{2,1,0:T(4,128)(2,1)} %dot_general.15), kind=kOutput, calls=%fused_computation.1 | convolution fusion | flops 536870912 | bytes 8454144 | tf_op jit(solution)/shard_map/dot_general | solution.py:310
  96.1 0.7 copy.32.parts
  96.7 16.3 %shard_map.122 = f32[32,4,128]{2,1,0:T(4,128)} custom-call(f32[32,4,128]{2,1,0:T(4,128)} %copy.32.parts), custom_call_target="tpu_custom_call" | custom-call | tf_op jit(solution)/shard_map/pallas_call | solution.py:313
  113.1 0.9 reduce_sum.55
  113.9 0.6 broadcast_multiply_fusion.1
  114.5 0.1 div.46
  115.3 1.6 %select_reduce_fusion.1 = f32[]{:T(128)} fusion(f32[32,4,128]{2,1,0:T(4,128)} %shard_map.122, f32[]{:T(128)S(6)} %div.47, f32[32,4]{1,0:T(8,128)S(1)} %div.46, f32[128]{0:T(128)S(1)} %get-tuple-element.8, s32[32,4]{1,0:T(8,128)S(1)} %multiply_add_fusion), kind=kLoop, calls=%fused_computation.16 | loop fusion | flops 114687 | bytes 67080 | tf_op jit(solution)/shard_map/jit(trace)/reduce_sum | solution.py:236
  117.6 0.9 select_add_fusion
  118.5 0.1 copy.33
  118.6 0.9 fusion.6
  119.5 11.7 %cholesky.16 = f32[128,128]{1,0:T(8,128)S(1)} custom-call(f32[128,128]{1,0:T(8,128)S(1)} %fusion.6), custom_call_target="Cholesky" | custom-call | tf_op jit(solution)/shard_map/jit(cholesky)/cholesky | solution.py:238
  131.3 0.6 compare_reduce_fusion
  131.9 0.7 fusion.3
  132.6 9.8 %custom-call.8 = f32[1,128,128]{1,2,0:T(8,128)S(1)} custom-call(f32[1,128,128]{2,1,0:T(8,128)S(1)} %fusion.3), custom_call_target="InvertDiagBlocksLowerTriangular" | custom-call | tf_op jit(solution)/shard_map/triangular_solve | solution.py:241
  142.4 0.0 copy-done
  142.4 0.6 reduce_sum.58
  143.7 0.1 reshape.106
  143.8 0.1 reshape.110
  143.9 0.2 convolution_bitcast_fusion.1
  144.7 0.8 fusion.14
  146.2 0.1 mul.51
  146.3 3.1 %multiply_reduce_fusion = f32[128,128]{1,0:T(8,128)S(1)} fusion(bf16[8,4,4,128,128]{4,3,2,1,0:T(8,128)(2,1)} %shard_map.121, f32[8,4,4]{2,1,0:T(4,128)S(1)} %mul.51), kind=kLoop, calls=%fused_computation | loop fusion | flops 6275072 | bytes 4260352 | tf_op jit(solution)/shard_map/reduce_sum | solution.py:332
  149.4 0.6 slice_bitcast_fusion
  150.0 0.1 mul.54
  150.2 0.6 reshape.108
  (8 shorter events, 0.1 us)
Async XLA Ops:
  89.3 53.1 %copy-start = (f32[128]{0:T(128)S(1)}, f32[128]{0:T(128)}, u32[]{:S(2)}) copy-start(f32[128]{0:T(128)} %param.11) | copy-start | bytes 1540

commit v3 on v2

--- a/solution.py
+++ b/solution.py
@@ -88,14 +88,19 @@
     mine,
     embed,
     position,
+    value,
+    mixing,
+    out,
+    up,
+    down,
+    readout,
+    jac,
+    position_t,
     value_t,
-    mixing,
     out_t,
     up_t,
     down_t,
-    down,
-    readout,
-    jac,
+    readout_t,
     spins,
     stage,
     wide,
@@ -153,6 +158,12 @@
 
     lax.fori_loop(1, n_chain, start_spins, 0)
     spins[z] = mine[...]
+    position_t[...] = position[...].astype(jnp.float32).T
+    value_t[...] = value[...].T
+    out_t[...] = out[...].T
+    up_t[...] = up[...].T
+    down_t[...] = down[...].T
+    readout_t[...] = jnp.broadcast_to(readout[...], readout_t.shape[::-1]).T
     slab = pl.ds(pl.multiple_of(z * depth, depth), depth)
 
     def one_group(step, carry):
@@ -161,9 +172,9 @@
             spin_copy(step).wait_recv()
 
         g = lax.rem(z + step, n_chain)
-        base = position[...].astype(jnp.float32)
+        base = position_t[...]
         triple = jnp.concatenate([spins[g]] * 3, axis=0)
-        embedded = [dot(embed[k], triple) + base for k in range(group)]
+        embedded = [dot(embed[k], triple, ((0,), (0,))) + base for k in range(group)]
         values = [dot(value_t[...], norm_columns(e)).astype(jnp.bfloat16) for e in embedded]
         mixed = []
         for h in range(heads):
@@ -192,7 +203,7 @@
                     * (slope + (3.0 * slope * cubic) * squared)
                 )
                 output = output + dot(down_t[:, rows], hidden)
-            cotangent = (readout[...] * jnp.tanh(output)).astype(jnp.bfloat16)
+            cotangent = (readout_t[...] * jnp.tanh(output)).astype(jnp.bfloat16)
             wide[k % 2, 0] = features
             wide[k % 2, 1] = cotangent
             left, right = wide[k % 2, 0, slab, :], wide[k % 2, 1, slab, :]
@@ -230,6 +241,64 @@
         return carry
 
     lax.fori_loop(0, n_chain * group * (n_param - 1), end_slices, 0)
+
+
+def solve_kernel(raw, energy, solved):
+    size = raw.shape[0]
+    tile = 8
+    gram = raw[...]
+    by_row = jnp.mean(gram, axis=0, keepdims=True)
+    by_column = jnp.mean(gram, axis=1, keepdims=True)
+    gram = (gram - by_row - by_column + jnp.mean(by_row, axis=1, keepdims=True)) * (1.0 / size)
+    row = lax.broadcasted_iota(jnp.int32, (size, size), 0)
+    column = lax.broadcasted_iota(jnp.int32, (size, size), 1)
+    same = row == column
+    diagonal = jnp.sum(jnp.where(same, gram, 0.0), axis=0, keepdims=True)
+    scale = jnp.sum(diagonal, axis=1, keepdims=True) * (1.0 / size)
+    system = gram + jnp.where(same, damping * scale, 0.0)
+    right = jnp.broadcast_to(energy[...], (size, size)).T
+    rest = jnp.concatenate([system, right], axis=1)
+    sub = lax.broadcasted_iota(jnp.int32, (tile, size), 0)
+    lane = lax.broadcasted_iota(jnp.int32, (tile, size), 1)
+
+    def across(block, i):
+        return jnp.broadcast_to(block[i : i + 1], block.shape)
+
+    saved = []
+    for start in range(0, size, tile):
+        left, aim = rest[:tile, :size], rest[:tile, size:]
+        columns = [
+            jnp.broadcast_to(left[:, start + j : start + j + 1], (tile, size)) for j in range(tile)
+        ]
+        inverse = jnp.zeros((tile, size), jnp.float32)
+        for i in range(tile):
+            over = 1.0 / across(columns[i], i)
+            inverse = jnp.where(sub == i, over, inverse)
+            factor = jnp.where(sub > i, columns[i] * over, 0.0)
+            left = left - factor * across(left, i)
+            aim = aim - factor * across(aim, i)
+            for j in range(i + 1, tile):
+                columns[j] = columns[j] - factor * across(columns[j], i)
+        saved.append((left, aim, columns, inverse))
+        if start + tile < size:
+            scaled = jnp.concatenate([left * inverse, aim * inverse], axis=1)
+            taken = lax.dot_general(
+                left,
+                scaled,
+                (((0,), (0,)), ((), ())),
+                precision=lax.Precision.HIGHEST,
+                preferred_element_type=jnp.float32,
+            )
+            rest = rest[tile:] - taken[start + tile :]
+    answer = jnp.zeros((tile, size), jnp.float32)
+    for start in range(size - tile, -1, -tile):
+        left, aim, columns, inverse = saved[start // tile]
+        aim = aim - jnp.sum(left * answer, axis=1, keepdims=True)
+        for i in range(tile - 1, -1, -1):
+            found = across(aim * inverse, i)
+            answer = jnp.where(lane == start + i, found, answer)
+            aim = aim - columns[i] * found
+    solved[...] = answer[:1] * scale
 
 
 def solve_weights(gram, energy, total):
@@ -273,7 +342,8 @@
     low = embed_weight - high - middle
     parts = jnp.stack([high, middle, low]).astype(jnp.bfloat16)
     pick = jnp.eye(samples, dtype=jnp.bfloat16)
-    embed = jnp.einsum("kg,acd->kdagc", pick, parts).reshape(samples, width, 3 * samples * sites)
+    embed = pick[:, None, :, None, None] * parts[:, None, :, :]
+    embed = embed.reshape(samples, 3 * samples * sites, width)
 
     sems = (n_chain, samples, n_param)
     jac = pl.pallas_call(
@@ -281,9 +351,15 @@
         out_shape=jax.ShapeDtypeStruct(
             (n_param, n_chain, samples, 2 * depth, shard), jnp.bfloat16
         ),
-        in_specs=[vmem] * 10,
+        in_specs=[vmem] * 9,
         out_specs=vmem,
         scratch_shapes=[
+            pltpu.VMEM((width, patches), jnp.float32),
+            pltpu.VMEM((width, width), jnp.bfloat16),
+            pltpu.VMEM((width, width), jnp.bfloat16),
+            pltpu.VMEM((hidden_units, width), jnp.bfloat16),
+            pltpu.VMEM((width, hidden_units), jnp.bfloat16),
+            pltpu.VMEM((width, patches), jnp.float32),
             pltpu.VMEM((n_chain, samples * sites, patches), jnp.bfloat16),
             pltpu.VMEM((n_chain, samples, n_param, 2 * depth, shard), jnp.bfloat16),
             pltpu.VMEM((2, 2, width, patches), jnp.bfloat16),
@@ -297,16 +373,15 @@
     )(
         signs,
         embed,
-        position.T,
-        value_weight.T,
+        position,
+        value_weight,
         mixing,
-        out_weight.T,
-        up_weight.T,
-        down_weight.T,
+        out_weight,
+        up_weight,
         down_weight,
-        readout[:, None],
+        readout[None, :],
     )
-    rows = jac.reshape(total, 2 * depth * shard)
+    rows = lax.optimization_barrier(jac.reshape(total, 2 * depth * shard))
     raw = lax.dot_general(
         rows, rows, (((1,), (1,)), ((), ())), preferred_element_type=jnp.float32
     )
@@ -322,11 +397,20 @@
         ],
         compiler_params=pltpu.CompilerParams(collective_id=1, has_side_effects=True),
     )(raw.reshape(count, samples, total)).reshape(total, total)
-    average = jnp.mean(raw, axis=0)
-    gram = (raw - average[None, :] - average[:, None] + jnp.mean(average)) / total
     energy = (local_energy - jnp.mean(local_energy)) / math.sqrt(total)
     energy = energy.reshape(n_chain, n_param, samples).swapaxes(0, 1).reshape(total)
-    solved = solve_weights(gram, energy, total)
+    if total <= 128 and total % 8 == 0:
+        solved = pl.pallas_call(
+            solve_kernel,
+            out_shape=jax.ShapeDtypeStruct((1, total), jnp.float32),
+            in_specs=[vmem, vmem],
+            out_specs=vmem,
+            compiler_params=pltpu.CompilerParams(vmem_limit_bytes=24 * 2**20),
+        )(raw, energy[None, :])[0]
+    else:
+        average = jnp.mean(raw, axis=0)
+        gram = (raw - average[None, :] - average[:, None] + jnp.mean(average)) / total
+        solved = solve_weights(gram, energy, total)
     sample_weights = solved.reshape(n_param, n_chain, samples).swapaxes(0, 1).reshape(total)
     pull = (solved - jnp.mean(solved)) * (-1.0 / math.sqrt(total))
     update = jnp.sum(pull[:, None] * rows.astype(jnp.float32), axis=0).reshape(2, depth, shard)

time: 152 us -> 109 us (0.72)
  other arithmetic: 33 us -> 7.22 us
  local copies, waits for them, and re-layouts: 29 us -> 9.47 us
  Pallas kernels: 77 us -> 87.9 us
  matrix products: 7.75 us -> 1.94 us
  between operations: 4.08 us -> 2.07 us
    another operation x6 -> x0, other arithmetic: 22.9 us -> none  [the longest x3 12.4 us: solve_weights(): lower = jnp.linalg.cholesky(system)]
    pallas_call x0 -> x1, Pallas kernels: none -> 10.4 us  [body(): pl.pallas_call(solve_kernel, out_shape=jax.ShapeDtypeStruct((1, total), j...]
    reshape x2 -> x0, local copies, waits for them, and re-layouts: 8.17 us -> none  [the longest x1 7.31 us: body(): rows = jac.reshape(total, 2 * depth * shard)]
    dot_general x2 -> x0, local copies, waits for them, and re-layouts: 7.75 us -> none  [body(): lax.dot_general(rows, rows, (((1,), (1,)), ((), ())), preferred_element_t...]
    dot_general x1, matrix products: 6.77 us -> 1.94 us  [body(): lax.dot_general(rows, rows, (((1,), (1,)), ((), ())), preferred_element_t...]
    unnamed x7, local copies, waits for them, and re-layouts: 9.1 us -> 6.58 us
    reduce_sum x2 -> x0, other arithmetic: 2.47 us -> none  [the longest x1 1.58 us: solve_weights(): scale = jnp.trace(gram) / total]
    div x2 -> x0, other arithmetic: 1.53 us -> none  [the longest x1 0.93 us: solve_weights(): lower = jnp.linalg.cholesky(system)]
where the time goes in v3:
time: 109 us
  Pallas kernels  87.9 us (81%)
  local copies, waits for them, and re-layouts  9.47 us (9%)
  other arithmetic  7.22 us (7%)
  between operations  2.07 us (2%)
  matrix products  1.94 us (2%)
    pallas_call x1, Pallas kernels, body(): pl.pallas_call(functools.partial(forward_kernel, n_chain, n_param), out_s...  61 us
    pallas_call x1, Pallas kernels, body(): pl.pallas_call(functools.partial(sum_kernel, count, n_param), out_shape=j...  16.5 us
    pallas_call x1, Pallas kernels, body(): pl.pallas_call(solve_kernel, out_shape=jax.ShapeDtypeStruct((1, total), j...  10.4 us
    unnamed x7, local copies, waits for them, and re-layouts  6.58 us
    reduce_sum x1, other arithmetic, body(): jnp.sum(pull[:, None] * rows.astype(jnp.float32), axis=0)  3.18 us

profile of v3, /device:TPU:1, one launch (start us, length us, event | category | flops | bytes accessed | tf_op | source)
XLA Modules:
  0.0 108.6 jit_solution(6201255706222427694)
XLA Ops:
  0.6 0.7 fusion.3
  1.4 0.1 mul.51
  1.5 0.1 mul.52
  1.6 0.7 broadcast_multiply_fusion.embed
  2.3 0.7 fusion
  3.0 0.6 reshape.94.mine
  3.6 61.0 %shard_map.121 = bf16[8,4,4,128,128]{4,3,2,1,0:T(8,128)(2,1)} custom-call(bf16[16,256]{1,0:T(8,128)(2,1)} %reshape.94.mine, bf16[4,48,256]{2,1,0:T(8,128)(2,1)} %broadcast_multiply_fusion.embed, bf16[256,256]{1,0:T(8,128)(2,1)} %position.1, bf16[256,256]{1,0:T(8,128)(2,1)} %value.1, bf16[8,256,256]{2,1,0:T(8,128)(2,1)} %mixing.1, bf16[256,256]{1,0:T(8,128)(2,1)} %out.1, ...), custom_call_target="tpu_custom_call" | custom-call | tf_op jit(solution)/shard_map/pallas_call | solution.py:349
  64.6 5.7 %copy.19 = bf16[16,8,128,128]{3,1,2,0:T(8,128)(2,1)S(1)} copy(bf16[16,8,128,128]{3,2,1,0:T(8,128)(2,1)} %bitcast.31) | data formatting | bytes 8388608
  70.4 0.0 copy-start.1
  70.4 0.0 copy-start.2
  70.4 1.9 %fusion.7 = f32[128,128]{1,0:T(8,128)} fusion(bf16[128,16384]{1,0:T(8,128)(2,1)S(1)} %bitcast.29), kind=kOutput, calls=%fused_computation.21 | convolution fusion | flops 536870912 | bytes 4259840 | tf_op jit(solution)/shard_map/dot_general | solution.py:385
  72.3 0.0 copy-done.1
  72.3 16.5 %shard_map.122 = f32[32,4,128]{2,1,0:T(4,128)} custom-call(f32[32,4,128]{2,1,0:T(4,128)} %bitcast.32), custom_call_target="tpu_custom_call" | custom-call | tf_op jit(solution)/shard_map/pallas_call | solution.py:388
  88.8 0.0 copy-done.2
  88.8 0.6 reduce_sum.27
  90.1 0.1 reshape.98
  90.2 0.1 broadcast_in_dim_reshape.3.energy
  90.3 0.0 copy-start
  90.3 0.8 copy-done
  91.2 10.4 %shard_map.123 = f32[1,128]{1,0:T(1,128)S(1)} custom-call(f32[128,128]{1,0:T(8,128)S(1)} %bitcast.28, f32[1,128]{1,0:T(1,128)S(1)} %broadcast_in_dim_reshape.3.energy), custom_call_target="tpu_custom_call" | custom-call | tf_op jit(solution)/shard_map/pallas_call | solution.py:403
  101.6 0.5 broadcast.25
  102.1 1.2 %fusion.6 = (f32[128]{0:T(128)S(1)}, f32[]{:T(128)}) fusion(f32[1,128]{1,0:T(1,128)S(1)} %shard_map.123, f32[]{:T(128)} %broadcast.25), kind=kLoop, calls=%fused_computation.20 | loop fusion | flops 127 | bytes 1032 | tf_op jit(solution)/shard_map/pallas_call | solution.py:403
  104.0 3.2 %multiply_reduce_fusion = f32[16384]{0:T(1024)S(1)} fusion(bf16[128,16384]{1,0:T(8,128)(2,1)} %bitcast.30, f32[128]{0:T(128)S(1)} %multiply_bitcast_fusion), kind=kLoop, calls=%fused_computation | loop fusion | flops 6275072 | bytes 4260352 | tf_op jit(solution)/shard_map/reduce_sum | solution.py:416
  107.2 0.6 slice_bitcast_fusion
  107.8 0.1 reshape_squeeze.3
  107.9 0.6 reshape.99
  (8 shorter events, 0.1 us)
Async XLA Ops:
  70.4 2.0 %copy-start.1 = (bf16[16,8,128,128]{3,1,2,0:T(8,128)(2,1)}, bf16[16,8,128,128]{3,1,2,0:T(8,128)(2,1)S(1)}, u32[]{:S(2)}) copy-start(bf16[16,8,128,128]{3,1,2,0:T(8,128)(2,1)S(1)} %copy.19) | copy-start | bytes 12582916
  70.4 18.4 %copy-start.2 = (f32[128]{0:T(128)S(1)}, f32[128]{0:T(128)}, u32[]{:S(2)}) copy-start(f32[128]{0:T(128)} %param.11) | copy-start | bytes 1540
  90.3 0.8 copy-start

commit v4 on v3

--- a/solution.py
+++ b/solution.py
@@ -25,61 +25,65 @@
     return (centred * lax.rsqrt(spread + 1e-05)).astype(jnp.bfloat16)
 
 
-def greet(count, peer_of):
+def sum_kernel(n_chain, n_param, parts, out, landed, passed, total, sems):
+    z, p = lax.axis_index("chain"), lax.axis_index("param")
     barrier = pltpu.get_barrier_semaphore()
 
-    def tell(k, carry):
-        pl.semaphore_signal(barrier, inc=1, device_id=peer_of(k), device_id_type=MESH)
-        return carry
-
-    lax.fori_loop(1, count, tell, 0)
-    pl.semaphore_wait(barrier, count - 1)
-
-
-def sum_kernel(count, per_row, parts, out, landed, total, sems):
-    z, p = lax.axis_index("chain"), lax.axis_index("param")
-    me = z * per_row + p
-
-    def peer_of(k):
-        q = lax.rem(me + k, count)
-        return (q // per_row, lax.rem(q, per_row))
-
-    greet(count, peer_of)
-
-    def scatter(k):
+    def in_plane(k):
+        return (z, lax.rem(p + k, n_param))
+
+    def in_chain(k):
+        return (lax.rem(z + k, n_chain), p)
+
+    def tell_plane(k, carry):
+        pl.semaphore_signal(barrier, inc=1, device_id=in_plane(k), device_id_type=MESH)
+        return carry
+
+    def tell_chain(k, carry):
+        pl.semaphore_signal(barrier, inc=1, device_id=in_chain(k), device_id_type=MESH)
+        return carry
+
+    lax.fori_loop(1, n_param, tell_plane, 0)
+    lax.fori_loop(1, n_chain, tell_chain, 0)
+    pl.semaphore_wait(barrier, n_chain + n_param - 2)
+
+    def copy(source, target, phase, k, there):
         return pltpu.make_async_remote_copy(
-            src_ref=parts.at[lax.rem(me + k, count)],
-            dst_ref=landed.at[me],
-            send_sem=sems.at[0, k],
-            recv_sem=sems.at[1, k],
-            device_id=peer_of(k),
+            src_ref=source,
+            dst_ref=target,
+            send_sem=sems.at[phase, 0, k],
+            recv_sem=sems.at[phase, 1, k],
+            device_id=there,
             device_id_type=MESH,
         )
 
+    def scatter(k):
+        return copy(parts.at[lax.rem(p + k, n_param)], landed.at[p], 0, k, in_plane(k))
+
+    def exchange(k):
+        return copy(total.at[0], passed.at[z], 1, k, in_chain(k))
+
     def spread(k):
-        return pltpu.make_async_remote_copy(
-            src_ref=total,
-            dst_ref=out.at[me],
-            send_sem=sems.at[2, k],
-            recv_sem=sems.at[3, k],
-            device_id=peer_of(k),
-            device_id_type=MESH,
-        )
-
-    def run(make, verb):
+        return copy(total.at[1], out.at[p], 2, k, in_plane(k))
+
+    def run(count, make, verb):
         def step(k, carry):
             getattr(make(k), verb)()
             return carry
 
         lax.fori_loop(1, count, step, 0)
 
-    run(scatter, "start")
-    landed[me] = parts[me]
-    run(scatter, "wait")
-    total[...] = jnp.sum(landed[...], axis=0)
-    run(spread, "start")
-    out[me] = total[...]
-    run(spread, "wait")
+    run(n_param, scatter, "start")
+    landed[p] = parts[p]
+    run(n_param, scatter, "wait")
+    total[0] = jnp.sum(landed[...], axis=0)
+    run(n_chain, exchange, "start")
+    passed[z] = total[0]
+    run(n_chain, exchange, "wait")
+    total[1] = jnp.sum(passed[...], axis=0)
+    run(n_param, spread, "start")
+    out[p] = total[1]
+    run(n_param, spread, "wait")
 
 
 def forward_kernel(
@@ -331,7 +335,6 @@
     total = local_energy.shape[0]
     width, hidden_units = up_weight.shape
     heads = mixing.shape[0]
-    count = n_chain * n_param
     depth, shard = width // n_chain, hidden_units // n_param
     vmem = pl.BlockSpec(memory_space=pltpu.VMEM)
 
@@ -385,18 +388,22 @@
     raw = lax.dot_general(
         rows, rows, (((1,), (1,)), ((), ())), preferred_element_type=jnp.float32
     )
+    share = total // n_param
     raw = pl.pallas_call(
-        functools.partial(sum_kernel, count, n_param),
-        out_shape=jax.ShapeDtypeStruct((count, samples, total), jnp.float32),
+        functools.partial(sum_kernel, n_chain, n_param),
+        out_shape=jax.ShapeDtypeStruct((n_param, share, total), jnp.float32),
         in_specs=[vmem],
         out_specs=vmem,
         scratch_shapes=[
-            pltpu.VMEM((count, samples, total), jnp.float32),
-            pltpu.VMEM((samples, total), jnp.float32),
-            pltpu.SemaphoreType.DMA((4, count)),
+            pltpu.VMEM((n_param, share, total), jnp.float32),
+            pltpu.VMEM((n_chain, share, total), jnp.float32),
+            pltpu.VMEM((2, share, total), jnp.float32),
+            pltpu.SemaphoreType.DMA((3, 2, max(n_chain, n_param))),
         ],
-        compiler_params=pltpu.CompilerParams(collective_id=1, has_side_effects=True),
-    )(raw.reshape(count, samples, total)).reshape(total, total)
+        compiler_params=pltpu.CompilerParams(
+            collective_id=1, has_side_effects=True, vmem_limit_bytes=32 * 2**20
+        ),
+    )(raw.reshape(n_param, share, total)).reshape(total, total)
     energy = (local_energy - jnp.mean(local_energy)) / math.sqrt(total)
     energy = energy.reshape(n_chain, n_param, samples).swapaxes(0, 1).reshape(total)
     if total <= 128 and total % 8 == 0:

time: 109 us -> 105 us (0.963)
  Pallas kernels: 87.9 us -> 84.9 us
    pallas_call x1, Pallas kernels: 16.5 us -> 13.5 us  [body(): pl.pallas_call(functools.partial(sum_kernel, n_chain, n_param), out_shape...]
    unnamed x7 -> x5, local copies, waits for them, and re-layouts: 6.58 us -> 6.39 us
where the time goes in v4:
time: 105 us
  Pallas kernels  84.9 us (81%)
  local copies, waits for them, and re-layouts  9.29 us (9%)
  other arithmetic  7.22 us (7%)
  between operations  2.07 us (2%)
  matrix products  1.24 us (1%)
    pallas_call x1, Pallas kernels, body(): pl.pallas_call(functools.partial(forward_kernel, n_chain, n_param), out_s...  61 us
    pallas_call x1, Pallas kernels, body(): pl.pallas_call(functools.partial(sum_kernel, n_chain, n_param), out_shape...  13.5 us
    pallas_call x1, Pallas kernels, body(): pl.pallas_call(solve_kernel, out_shape=jax.ShapeDtypeStruct((1, total), j...  10.4 us
    unnamed x5, local copies, waits for them, and re-layouts  6.39 us
    reduce_sum x1, other arithmetic, body(): jnp.sum(pull[:, None] * rows.astype(jnp.float32), axis=0)  3.18 us

profile of v4, /device:TPU:1, one launch (start us, length us, event | category | flops | bytes accessed | tf_op | source)
XLA Modules:
  0.0 104.7 jit_solution(16030563522144166782)
XLA Ops:
  0.6 0.7 fusion.3
  1.4 0.1 mul.51
  1.5 0.1 mul.52
  1.6 0.7 broadcast_multiply_fusion.embed
  2.3 0.7 fusion
  3.0 0.6 reshape.94.mine
  3.6 61.0 %shard_map.121 = bf16[8,4,4,128,128]{4,3,2,1,0:T(8,128)(2,1)} custom-call(bf16[16,256]{1,0:T(8,128)(2,1)} %reshape.94.mine, bf16[4,48,256]{2,1,0:T(8,128)(2,1)} %broadcast_multiply_fusion.embed, bf16[256,256]{1,0:T(8,128)(2,1)} %position.1, bf16[256,256]{1,0:T(8,128)(2,1)} %value.1, bf16[8,256,256]{2,1,0:T(8,128)(2,1)} %mixing.1, bf16[256,256]{1,0:T(8,128)(2,1)} %out.1, ...), custom_call_target="tpu_custom_call" | custom-call | tf_op jit(solution)/shard_map/pallas_call | solution.py:352
  64.6 5.7 %copy.19 = bf16[16,8,128,128]{3,1,2,0:T(8,128)(2,1)S(1)} copy(bf16[16,8,128,128]{3,2,1,0:T(8,128)(2,1)} %bitcast.32) | data formatting | bytes 8388608
  70.4 0.0 copy-start
  70.4 0.0 copy-start.1
  70.4 1.2 %fusion.7 = f32[128,128]{1,0:T(8,128)S(1)} fusion(bf16[128,16384]{1,0:T(8,128)(2,1)S(1)} %bitcast.30), kind=kOutput, calls=%fused_computation.21 | convolution fusion | flops 536870912 | bytes 4259840 | tf_op jit(solution)/shard_map/dot_general | solution.py:388
  71.7 0.7 copy-done
  72.3 13.5 %shard_map.122 = f32[8,16,128]{2,1,0:T(8,128)S(1)} custom-call(f32[8,16,128]{2,1,0:T(8,128)S(1)} %bitcast.28), custom_call_target="tpu_custom_call" | custom-call | tf_op jit(solution)/shard_map/pallas_call | solution.py:392
  85.8 0.0 copy-done.1
  85.9 0.6 reduce_sum.27
  87.1 0.1 reshape.98
  87.2 0.1 broadcast_in_dim_reshape.3.energy
  87.3 10.4 %shard_map.123 = f32[1,128]{1,0:T(1,128)S(1)} custom-call(f32[128,128]{1,0:T(8,128)S(1)} %bitcast.29, f32[1,128]{1,0:T(1,128)S(1)} %broadcast_in_dim_reshape.3.energy), custom_call_target="tpu_custom_call" | custom-call | tf_op jit(solution)/shard_map/pallas_call | solution.py:410
  97.8 0.5 broadcast.25
  98.3 1.2 %fusion.6 = (f32[128]{0:T(128)S(1)}, f32[]{:T(128)}) fusion(f32[1,128]{1,0:T(1,128)S(1)} %shard_map.123, f32[]{:T(128)} %broadcast.25), kind=kLoop, calls=%fused_computation.20 | loop fusion | flops 127 | bytes 1032 | tf_op jit(solution)/shard_map/pallas_call | solution.py:410
  100.2 3.2 %multiply_reduce_fusion = f32[16384]{0:T(1024)S(1)} fusion(bf16[128,16384]{1,0:T(8,128)(2,1)} %bitcast.31, f32[128]{0:T(128)S(1)} %multiply_bitcast_fusion), kind=kLoop, calls=%fused_computation | loop fusion | flops 6275072 | bytes 4260352 | tf_op jit(solution)/shard_map/reduce_sum | solution.py:423
  103.4 0.6 slice_bitcast_fusion
  104.0 0.1 reshape_squeeze.3
  104.1 0.6 reshape.99
  (8 shorter events, 0.1 us)
Async XLA Ops:
  70.4 1.9 %copy-start = (bf16[16,8,128,128]{3,1,2,0:T(8,128)(2,1)}, bf16[16,8,128,128]{3,1,2,0:T(8,128)(2,1)S(1)}, u32[]{:S(2)}) copy-start(bf16[16,8,128,128]{3,1,2,0:T(8,128)(2,1)S(1)} %copy.19) | copy-start | bytes 12582916
  70.4 15.5 %copy-start.1 = (f32[128]{0:T(128)S(1)}, f32[128]{0:T(128)}, u32[]{:S(2)}) copy-start(f32[128]{0:T(128)} %param.11) | copy-start | bytes 1540
